TPU v7x, 256 devices: a whole 4x4x8 slice. The times are simulated.
256 devices in a mesh: tm: 4 (over y), height: 4 (over x), width: 16 (over z, core).
Axes of the slice: x: 4, y: 4, z: 8, core: 2. Of those that a mesh axis runs over, the one named last changes fastest.
Arguments:
- features: bfloat16 [16, 32, 160, 384], P('tm', 'height', 'width'), may hold values from -6 to 6
- first_gain: float32 [384], replicated, may hold values from 0.5 to 2
- first_kernel: bfloat16 [27, 384, 384], P(None, ('height', 'width')), may hold values from -0.0625 to 0.0625
- first_bias: float32 [384], replicated, may hold values from -3 to 3
- second_gain: float32 [384], replicated, may hold values from 0.5 to 2
- second_kernel: bfloat16 [27, 384, 384], P(None, ('height', 'width')), may hold values from -0.0625 to 0.0625
- second_bias: float32 [384], replicated, may hold values from -3 to 3
Outputs:
- block_out: bfloat16 [16, 32, 160, 384], P('tm', 'height', 'width')
All inputs are finite; a program needn't handle non-finite values.
Results may differ from a plain program's by a relative error of at most 0.012.
Values may be sent and summed in bfloat16 or wider, within the bound.
No kernel may reach another device: no remote copies, remote signals or barrier semaphores. Data moves between devices by JAX's collectives and lax.ppermute only.
A program may use at most 128 MiB of HBM per device.

v0:
```python
import jax
import jax.numpy as jnp
from jax import lax
from jax.sharding import PartitionSpec as P


def passed_along(x, axis, by):
    devices = lax.axis_size(axis)
    pairs = [(i, i + by) for i in range(devices) if 0 <= i + by < devices]
    return lax.ppermute(x, axis, pairs)


def extended(x, sides, width):
    for axis, dim in sides:
        devices, length = (lax.axis_size(axis), x.shape[dim])
        up = [(i, (i + 1) % devices) for i in range(devices - 1)]
        down = [(j, i) for i, j in up]
        last = lax.slice_in_dim(x, length - width, length, axis=dim)
        first = lax.slice_in_dim(x, 0, width, axis=dim)
        before = lax.ppermute(last, axis, up)
        after = lax.ppermute(first, axis, down)
        x = jnp.concatenate([before, x, after], axis=dim)
    return x


def activate(volume, gain):
    values = volume.astype(jnp.float32)
    square_mean = jnp.mean(values * values, axis=-1, keepdims=True)
    normed = values * lax.rsqrt(square_mean + 1e-06) * gain
    return jax.nn.silu(normed).astype(jnp.bfloat16)


def make_folder(widened, frames, rows, cols):

    def fold_piece(total, piece, start):
        count_in = piece.shape[1]
        for step_t in range(3):
            for step_h in range(3):
                for step_w in range(3):
                    window = widened[
                        step_t : step_t + frames, step_h : step_h + rows, step_w : step_w + cols
                    ]
                    total = total + jnp.dot(
                        window.reshape(-1, count_in),
                        piece[9 * step_t + 3 * step_h + step_w],
                        preferred_element_type=jnp.float32,
                    )
        return total

    return fold_piece


def convolve(widened, kernel, bias, frames, rows, cols):
    out_chans = kernel.shape[2]
    empty = jnp.zeros((frames * rows * cols, out_chans), jnp.float32)
    fold_piece = make_folder(widened, frames, rows, cols)
    row_kernel = lax.all_gather(kernel, "width", axis=1, tiled=True)
    total = fold_piece(
        empty, lax.all_gather(row_kernel, "height", axis=1, tiled=True), jnp.int32(0)
    )
    return total.reshape(frames, rows, cols, out_chans) + bias


def widen(active):
    earlier = passed_along(active[-2:], "tm", 1)
    tall = jnp.concatenate([earlier, active], axis=0)
    return extended(tall, (("height", 1), ("width", 2)), 1)


def on_device(
    features, first_gain, first_kernel, first_bias, second_gain, second_kernel, second_bias
):
    frames, rows, cols, chans = features.shape
    first_active = activate(features, first_gain)
    middle = convolve(widen(first_active), first_kernel, first_bias, frames, rows, cols).astype(
        jnp.bfloat16
    )
    second_active = activate(middle, second_gain)
    second_wide = widen(second_active)
    summed = convolve(
        second_wide, second_kernel, second_bias, frames, rows, cols
    ) + features.astype(jnp.float32)
    return summed.astype(jnp.bfloat16)


def solution(mesh):
    placed = (
        P("tm", "height", "width", None),
        P(),
        P(None, ("height", "width"), None),
        P(),
        P(),
        P(None, ("height", "width"), None),
        P(),
    )
    return jax.shard_map(
        on_device,
        mesh=mesh,
        in_specs=placed,
        out_specs=P("tm", "height", "width", None),
        check_vma=False,
    )
```

profile of v0, /device:TPU:1, one launch (start us, length us, event | category | flops | bytes accessed | tf_op | source)
XLA Modules:
  0.0 329.2 jit_solution(13650596367216335500)
XLA Ops:
  8.1 45.3 %all-gather.5.cloned.1.call-done = bf16[27,96,384]{2,0,1:T(8,128)(2,1)} async-done(((bf16[27,6,384]{2,0,1:T(8,128)(2,1)}), bf16[27,96,384]{2,0,1:T(8,128)(2,1)}) %all-gather.5.cloned.1.call-update) | async-done | bytes 1990672 | tf_op jit(solution)/shard_map/all_gather | solution.py:57
  53.4 3.7 %copy.15 = bf16[27,96,384]{2,1,0:T(8,128)(2,1)} copy(bf16[27,96,384]{2,0,1:T(8,128)(2,1)} %all-gather.5.cloned.1.call-done) | data formatting | bytes 3981312 | tf_op jit(solution)/shard_map/all_gather | solution.py:57
  57.1 36.5 %all-gather.9.cloned.1.call-done = bf16[27,96,384]{2,0,1:T(8,128)(2,1)} async-done(((bf16[27,6,384]{2,0,1:T(8,128)(2,1)}), bf16[27,96,384]{2,0,1:T(8,128)(2,1)}) %all-gather.9.cloned.1.call-update) | async-done | bytes 1990672 | tf_op jit(solution)/shard_map/all_gather | solution.py:57
  93.6 3.7 %copy.16 = bf16[27,96,384]{2,1,0:T(8,128)(2,1)} copy(bf16[27,96,384]{2,0,1:T(8,128)(2,1)} %all-gather.9.cloned.1.call-done) | data formatting | bytes 3981312 | tf_op jit(solution)/shard_map/all_gather | solution.py:57
  97.9 3.1 collective-permute-start
  101.8 3.2 collective-permute-done
  106.3 4.0 %collective-permute-start.1 = (bf16[6,1,10,384]{3,2,1,0:T(8,128)(2,1)S(1)}, bf16[6,1,10,384]{3,2,1,0:T(8,128)(2,1)S(1)}, u32[]{:S(2)}, u32[]{:S(2)}) collective-permute-start(bf16[6,1,10,384]{3,2,1,0:T(8,128)(2,1)S(1)} %get-tuple-element.71), channel_id=1, source_target_pairs={{0,16},{16,32},{32,48},{1,17},{17,33},{33,49},{2,18},{18,34},{34,5... | collective-permute-start | bytes 138248 | tf_op jit(solution)/shard_map/ppermute | solution.py:20
  114.2 4.9 %collective-permute-start.3 = (bf16[6,10,1,384]{3,2,1,0:T(2,128)(2,1)}, bf16[6,10,1,384]{3,2,1,0:T(2,128)(2,1)S(1)}, u32[]{:S(2)}, u32[]{:S(2)}) collective-permute-start(bf16[6,10,1,384]{3,2,1,0:T(2,128)(2,1)} %get-tuple-element.47), channel_id=1, source_target_pairs={{0,1},{1,2},{2,3},{3,4},{4,5},{5,6},{6,7},{7,8},{8,9},{9,10},{10,1... | collective-permute-start | bytes 138248 | tf_op jit(solution)/shard_map/ppermute | solution.py:20
  119.1 2.1 collective-permute-start.4
  127.2 2.3 fusion.32
  129.4 1.8 reshape.211
  131.2 1.8 reshape.197
  133.0 1.8 reshape.199
  134.8 1.8 reshape.200
  136.6 1.8 reshape.202
  138.4 1.8 reshape.203
  140.2 1.8 reshape.205
  142.0 1.8 reshape.206
  143.8 1.8 reshape.208
  145.6 1.8 reshape.209
  151.7 24.5 %all-gather.7.cloned.1.call-done = bf16[27,384,384]{2,1,0:T(8,128)(2,1)} async-done(((bf16[27,96,384]{2,1,0:T(8,128)(2,1)}), bf16[27,384,384]{2,1,0:T(8,128)(2,1)}) %all-gather.7.cloned.1.call-update) | async-done | bytes 7962640 | tf_op jit(solution)/shard_map/all_gather | solution.py:59
  176.2 1.6 fusion.23
  177.8 1.8 fusion.24
  179.5 1.4 convolution_add_fusion.49
  181.0 1.5 convolution_add_fusion.48
  182.4 1.5 convolution_add_fusion.47
  183.9 1.3 convolution_add_fusion.46
  186.4 1.3 convolution_add_fusion.42
  194.3 3.3 collective-permute-start.5
  197.6 3.5 %collective-permute-done.5 = bf16[2,8,10,384]{3,2,1,0:T(8,128)(2,1)S(1)} collective-permute-done((bf16[2,8,10,384]{3,2,1,0:T(8,128)(2,1)S(1)}, bf16[2,8,10,384]{3,2,1,0:T(8,128)(2,1)S(1)}, u32[]{:S(2)}, u32[]{:S(2)}) %collective-permute-start.5) | collective-permute-done | bytes 122912 | tf_op jit(solution)/shard_map/ppermute | solution.py:10
  202.5 4.2 %collective-permute-start.6 = (bf16[6,1,10,384]{3,2,1,0:T(8,128)(2,1)S(1)}, bf16[6,1,10,384]{3,2,1,0:T(8,128)(2,1)S(1)}, u32[]{:S(2)}, u32[]{:S(2)}) collective-permute-start(bf16[6,1,10,384]{3,2,1,0:T(8,128)(2,1)S(1)} %get-tuple-element.65), channel_id=1, source_target_pairs={{0,16},{16,32},{32,48},{1,17},{17,33},{33,49},{2,18},{18,34},{34,5... | collective-permute-start | bytes 138248 | tf_op jit(solution)/shard_map/ppermute | solution.py:20
  210.1 5.8 %collective-permute-start.8 = (bf16[6,10,1,384]{3,2,1,0:T(2,128)(2,1)}, bf16[6,10,1,384]{3,2,1,0:T(2,128)(2,1)}, u32[]{:S(2)}, u32[]{:S(2)}) collective-permute-start(bf16[6,10,1,384]{3,2,1,0:T(2,128)(2,1)} %get-tuple-element.25), channel_id=1, source_target_pairs={{0,1},{1,2},{2,3},{3,4},{4,5},{5,6},{6,7},{7,8},{8,9},{9,10},{10,1... | collective-permute-start | bytes 138248 | tf_op jit(solution)/shard_map/ppermute | solution.py:20
  215.9 1.9 collective-permute-start.9
  220.1 42.1 %all-gather.11.cloned.1.call-done = bf16[27,384,384]{2,1,0:T(8,128)(2,1)} async-done(((bf16[27,96,384]{2,1,0:T(8,128)(2,1)}), bf16[27,384,384]{2,1,0:T(8,128)(2,1)}) %all-gather.11.cloned.1.call-update) | async-done | bytes 7962640 | tf_op jit(solution)/shard_map/all_gather | solution.py:59
  262.2 1.4 fusion.22
  263.6 1.8 reshape.232
  266.2 1.8 reshape.241
  268.8 1.8 reshape.249
  270.5 1.6 maximum_maximum_fusion.1
  272.1 1.8 fusion.30
  273.9 1.8 reshape.239
  275.7 1.9 fusion.31
  277.6 1.9 reshape.225
  279.4 1.8 reshape.227
  281.2 1.8 reshape.228
  283.0 1.8 reshape.230
  284.8 1.8 reshape.231
  286.6 1.8 reshape.233
  288.4 1.8 reshape.234
  290.1 1.8 reshape.236
  291.9 1.8 reshape.237
  293.7 1.8 reshape.240
  295.5 1.8 reshape.242
  297.3 1.8 reshape.243
  300.3 1.6 fusion.21
  301.9 1.4 convolution_add_fusion.24
  303.3 1.5 convolution_add_fusion.23
  304.8 1.5 convolution_add_fusion.22
  306.2 1.5 convolution_add_fusion.21
  307.7 1.6 convolution_add_fusion.20
  309.3 1.5 convolution_add_fusion.19
  310.8 1.5 convolution_add_fusion.18
  312.2 1.5 convolution_add_fusion.17
  313.7 1.3 convolution_add_fusion.16
  (186 shorter events, 42.7 us)
Async XLA Ops:
  6.5 90.8 %copy-start.1 = (bf16[4,8,10,384]{3,1,2,0:T(8,128)(2,1)S(1)}, bf16[4,8,10,384]{3,1,2,0:T(8,128)(2,1)}, u32[]{:S(2)}) copy-start(bf16[4,8,10,384]{3,1,2,0:T(8,128)(2,1)} %param.7) | copy-start | bytes 737284
  6.5 91.0 %copy-start.35 = (f32[384]{0:T(512)S(1)}, f32[384]{0:T(512)}, u32[]{:S(2)}) copy-start(f32[384]{0:T(512)} %param.8) | copy-start | bytes 4612
  6.5 46.8 %all-gather.5.cloned.1.call-start = ((), (), s32[]{:S(2)}) async-start(), calls=%async_computation | async-start | bytes 2506752 | tf_op jit(solution)/shard_map/all_gather | solution.py:57
  7.3 86.4 %all-gather.9.cloned.1.call-start = ((), (), s32[]{:S(2)}) async-start(), calls=%async_computation.2 | async-start | bytes 2506752 | tf_op jit(solution)/shard_map/all_gather | solution.py:57
  8.0 168.2 %all-gather.7.cloned.1.call-start = ((), (), s32[]{:S(2)}) async-start(), calls=%async_computation.1 | async-start | bytes 9953280 | tf_op jit(solution)/shard_map/all_gather | solution.py:59
  57.1 205.1 %all-gather.11.cloned.1.call-start = ((), (), s32[]{:S(2)}) async-start(), calls=%async_computation.3 | async-start | bytes 9953280 | tf_op jit(solution)/shard_map/all_gather | solution.py:59
  97.9 7.1 %collective-permute-start = (bf16[2,8,10,384]{3,2,1,0:T(8,128)(2,1)S(1)}, bf16[2,8,10,384]{3,2,1,0:T(8,128)(2,1)S(1)}, u32[]{:S(2)}, u32[]{:S(2)}) collective-permute-start(bf16[2,8,10,384]{3,2,1,0:T(8,128)(2,1)S(1)} %slice.512), channel_id=1, source_target_pairs={{0,64},{64,128},{128,192},{1,65},{65,129},{129,193},{2,66},{66,130... | collective-permute-start | bytes 368648 | tf_op jit(solution)/shard_map/ppermute | solution.py:10
  105.0 7.0 %collective-permute-start.2 = (bf16[6,1,10,384]{3,2,1,0:T(8,128)(2,1)S(1)}, bf16[6,1,10,384]{3,2,1,0:T(8,128)(2,1)S(1)}, u32[]{:S(2)}, u32[]{:S(2)}) collective-permute-start(bf16[6,1,10,384]{3,2,1,0:T(8,128)(2,1)S(1)} %get-tuple-element.72), channel_id=1, source_target_pairs={{16,0},{32,16},{48,32},{17,1},{33,17},{49,33},{18,2},{34,18},{50,3... | collective-permute-start | bytes 138248 | tf_op jit(solution)/shard_map/ppermute | solution.py:21
  106.3 7.0 %collective-permute-start.1 = (bf16[6,1,10,384]{3,2,1,0:T(8,128)(2,1)S(1)}, bf16[6,1,10,384]{3,2,1,0:T(8,128)(2,1)S(1)}, u32[]{:S(2)}, u32[]{:S(2)}) collective-permute-start(bf16[6,1,10,384]{3,2,1,0:T(8,128)(2,1)S(1)} %get-tuple-element.71), channel_id=1, source_target_pairs={{0,16},{16,32},{32,48},{1,17},{17,33},{33,49},{2,18},{18,34},{34,5... | collective-permute-start | bytes 138248 | tf_op jit(solution)/shard_map/ppermute | solution.py:20
  114.2 12.3 %collective-permute-start.3 = (bf16[6,10,1,384]{3,2,1,0:T(2,128)(2,1)}, bf16[6,10,1,384]{3,2,1,0:T(2,128)(2,1)S(1)}, u32[]{:S(2)}, u32[]{:S(2)}) collective-permute-start(bf16[6,10,1,384]{3,2,1,0:T(2,128)(2,1)} %get-tuple-element.47), channel_id=1, source_target_pairs={{0,1},{1,2},{2,3},{3,4},{4,5},{5,6},{6,7},{7,8},{8,9},{9,10},{10,1... | collective-permute-start | bytes 138248 | tf_op jit(solution)/shard_map/ppermute | solution.py:20
  119.1 7.4 %collective-permute-start.4 = (bf16[6,10,1,384]{3,2,1,0:T(2,128)(2,1)}, bf16[6,10,1,384]{3,2,1,0:T(2,128)(2,1)S(1)}, u32[]{:S(2)}, u32[]{:S(2)}) collective-permute-start(bf16[6,10,1,384]{3,2,1,0:T(2,128)(2,1)} %get-tuple-element.48), channel_id=1, source_target_pairs={{1,0},{2,1},{3,2},{4,3},{5,4},{6,5},{7,6},{8,7},{9,8},{10,9},{11,1... | collective-permute-start | bytes 138248 | tf_op jit(solution)/shard_map/ppermute | solution.py:21
  148.1 35.8 %copy-start.7 = (bf16[320,384]{1,0:T(8,128)(2,1)S(1)}, bf16[320,384]{1,0:T(8,128)(2,1)}, u32[]{:S(2)}) copy-start(bf16[320,384]{1,0:T(8,128)(2,1)} %reshape.201) | copy-start | bytes 737284
  148.9 37.1 %copy-start.14 = (bf16[320,384]{1,0:T(8,128)(2,1)S(1)}, bf16[320,384]{1,0:T(8,128)(2,1)}, u32[]{:S(2)}) copy-start(bf16[320,384]{1,0:T(8,128)(2,1)} %reshape.204) | copy-start | bytes 737284
  151.4 36.3 %copy-start.26 = (bf16[320,384]{1,0:T(8,128)(2,1)S(1)}, bf16[320,384]{1,0:T(8,128)(2,1)}, u32[]{:S(2)}) copy-start(bf16[320,384]{1,0:T(8,128)(2,1)} %reshape.206) | copy-start | bytes 737284
  151.5 33.8 %copy-start.31 = (bf16[320,384]{1,0:T(8,128)(2,1)S(1)}, bf16[320,384]{1,0:T(8,128)(2,1)}, u32[]{:S(2)}) copy-start(bf16[320,384]{1,0:T(8,128)(2,1)} %reshape.202) | copy-start | bytes 737284
  151.5 34.2 %copy-start.29 = (bf16[320,384]{1,0:T(8,128)(2,1)S(1)}, bf16[320,384]{1,0:T(8,128)(2,1)}, u32[]{:S(2)}) copy-start(bf16[320,384]{1,0:T(8,128)(2,1)} %reshape.203) | copy-start | bytes 737284
  176.2 9.1 %copy-start = (bf16[27,384,384]{2,1,0:T(8,128)(2,1)S(1)}, bf16[27,384,384]{2,1,0:T(8,128)(2,1)}, u32[]{:S(2)}) copy-start(bf16[27,384,384]{2,1,0:T(8,128)(2,1)} %all-gather.7.cloned.1.call-done) | copy-start | bytes 23887876
  176.2 11.9 %copy-start.12 = (bf16[320,384]{1,0:T(8,128)(2,1)S(1)}, bf16[320,384]{1,0:T(8,128)(2,1)}, u32[]{:S(2)}) copy-start(bf16[320,384]{1,0:T(8,128)(2,1)} %reshape.207) | copy-start | bytes 737284
  177.8 10.7 %copy-start.25 = (bf16[320,384]{1,0:T(8,128)(2,1)S(1)}, bf16[320,384]{1,0:T(8,128)(2,1)}, u32[]{:S(2)}) copy-start(bf16[320,384]{1,0:T(8,128)(2,1)} %reshape.208) | copy-start | bytes 737284
  181.0 7.8 %copy-start.23 = (bf16[320,384]{1,0:T(8,128)(2,1)S(1)}, bf16[320,384]{1,0:T(8,128)(2,1)}, u32[]{:S(2)}) copy-start(bf16[320,384]{1,0:T(8,128)(2,1)} %reshape.209) | copy-start | bytes 737284
  182.4 6.7 %copy-start.33 = (bf16[320,384]{1,0:T(8,128)(2,1)S(1)}, bf16[320,384]{1,0:T(8,128)(2,1)}, u32[]{:S(2)}) copy-start(bf16[320,384]{1,0:T(8,128)(2,1)} %reshape.210) | copy-start | bytes 737284
  183.9 5.6 %copy-start.20 = (bf16[320,384]{1,0:T(8,128)(2,1)S(1)}, bf16[320,384]{1,0:T(8,128)(2,1)}, u32[]{:S(2)}) copy-start(bf16[320,384]{1,0:T(8,128)(2,1)} %reshape.212) | copy-start | bytes 737284
  185.3 4.5 %copy-start.10 = (bf16[320,384]{1,0:T(8,128)(2,1)S(1)}, bf16[320,384]{1,0:T(8,128)(2,1)}, u32[]{:S(2)}) copy-start(bf16[320,384]{1,0:T(8,128)(2,1)} %reshape.213) | copy-start | bytes 737284
  185.7 4.5 %copy-start.18 = (bf16[320,384]{1,0:T(8,128)(2,1)S(1)}, bf16[320,384]{1,0:T(8,128)(2,1)}, u32[]{:S(2)}) copy-start(bf16[320,384]{1,0:T(8,128)(2,1)} %reshape.214) | copy-start | bytes 737284
  186.0 4.5 %copy-start.17 = (bf16[320,384]{1,0:T(8,128)(2,1)S(1)}, bf16[320,384]{1,0:T(8,128)(2,1)}, u32[]{:S(2)}) copy-start(bf16[320,384]{1,0:T(8,128)(2,1)} %reshape.215) | copy-start | bytes 737284
  186.4 4.5 %copy-start.8 = (bf16[320,384]{1,0:T(8,128)(2,1)S(1)}, bf16[320,384]{1,0:T(8,128)(2,1)}, u32[]{:S(2)}) copy-start(bf16[320,384]{1,0:T(8,128)(2,1)} %reshape.216) | copy-start | bytes 737284
  187.7 3.5 %copy-start.16 = (bf16[320,384]{1,0:T(8,128)(2,1)S(1)}, bf16[320,384]{1,0:T(8,128)(2,1)}, u32[]{:S(2)}) copy-start(bf16[320,384]{1,0:T(8,128)(2,1)} %reshape.217) | copy-start | bytes 737284
  188.1 3.5 %copy-start.15 = (bf16[320,384]{1,0:T(8,128)(2,1)S(1)}, bf16[320,384]{1,0:T(8,128)(2,1)}, u32[]{:S(2)}) copy-start(bf16[320,384]{1,0:T(8,128)(2,1)} %reshape.218) | copy-start | bytes 737284
  188.4 3.5 %copy-start.4 = (bf16[320,384]{1,0:T(8,128)(2,1)S(1)}, bf16[320,384]{1,0:T(8,128)(2,1)}, u32[]{:S(2)}) copy-start(bf16[320,384]{1,0:T(8,128)(2,1)} %reshape.219) | copy-start | bytes 737284
  189.5 3.5 %copy-start.5 = (bf16[320,384]{1,0:T(8,128)(2,1)S(1)}, bf16[320,384]{1,0:T(8,128)(2,1)}, u32[]{:S(2)}) copy-start(bf16[320,384]{1,0:T(8,128)(2,1)} %reshape.222) | copy-start | bytes 737284
  189.9 3.5 %copy-start.34 = (f32[384]{0:T(512)S(1)}, f32[384]{0:T(512)}, u32[]{:S(2)}) copy-start(f32[384]{0:T(512)} %param.10) | copy-start | bytes 4612
  190.2 3.8 %copy-start.36 = (f32[384]{0:T(512)S(1)}, f32[384]{0:T(512)}, u32[]{:S(2)}) copy-start(f32[384]{0:T(512)} %param.11) | copy-start | bytes 4612
  194.3 6.8 %collective-permute-start.5 = (bf16[2,8,10,384]{3,2,1,0:T(8,128)(2,1)S(1)}, bf16[2,8,10,384]{3,2,1,0:T(8,128)(2,1)S(1)}, u32[]{:S(2)}, u32[]{:S(2)}) collective-permute-start(bf16[2,8,10,384]{3,2,1,0:T(8,128)(2,1)S(1)} %slice.566), channel_id=1, source_target_pairs={{0,64},{64,128},{128,192},{1,65},{65,129},{129,193},{2,66},{66,130... | collective-permute-start | bytes 368648 | tf_op jit(solution)/shard_map/ppermute | solution.py:10
  201.2 7.2 %collective-permute-start.7 = (bf16[6,1,10,384]{3,2,1,0:T(8,128)(2,1)S(1)}, bf16[6,1,10,384]{3,2,1,0:T(8,128)(2,1)S(1)}, u32[]{:S(2)}, u32[]{:S(2)}) collective-permute-start(bf16[6,1,10,384]{3,2,1,0:T(8,128)(2,1)S(1)} %get-tuple-element.66), channel_id=1, source_target_pairs={{16,0},{32,16},{48,32},{17,1},{33,17},{49,33},{18,2},{34,18},{50,3... | collective-permute-start | bytes 138248 | tf_op jit(solution)/shard_map/ppermute | solution.py:21
  202.5 6.8 %collective-permute-start.6 = (bf16[6,1,10,384]{3,2,1,0:T(8,128)(2,1)S(1)}, bf16[6,1,10,384]{3,2,1,0:T(8,128)(2,1)S(1)}, u32[]{:S(2)}, u32[]{:S(2)}) collective-permute-start(bf16[6,1,10,384]{3,2,1,0:T(8,128)(2,1)S(1)} %get-tuple-element.65), channel_id=1, source_target_pairs={{0,16},{16,32},{32,48},{1,17},{17,33},{33,49},{2,18},{18,34},{34,5... | collective-permute-start | bytes 138248 | tf_op jit(solution)/shard_map/ppermute | solution.py:20
  210.1 60.4 %collective-permute-start.8 = (bf16[6,10,1,384]{3,2,1,0:T(2,128)(2,1)}, bf16[6,10,1,384]{3,2,1,0:T(2,128)(2,1)}, u32[]{:S(2)}, u32[]{:S(2)}) collective-permute-start(bf16[6,10,1,384]{3,2,1,0:T(2,128)(2,1)} %get-tuple-element.25), channel_id=1, source_target_pairs={{0,1},{1,2},{2,3},{3,4},{4,5},{5,6},{6,7},{7,8},{8,9},{9,10},{10,1... | collective-permute-start | bytes 138248 | tf_op jit(solution)/shard_map/ppermute | solution.py:20
  215.9 54.6 %collective-permute-start.9 = (bf16[6,10,1,384]{3,2,1,0:T(2,128)(2,1)}, bf16[6,10,1,384]{3,2,1,0:T(2,128)(2,1)}, u32[]{:S(2)}, u32[]{:S(2)}) collective-permute-start(bf16[6,10,1,384]{3,2,1,0:T(2,128)(2,1)} %get-tuple-element.26), channel_id=1, source_target_pairs={{1,0},{2,1},{3,2},{4,3},{5,4},{6,5},{7,6},{8,7},{9,8},{10,9},{11,1... | collective-permute-start | bytes 138248 | tf_op jit(solution)/shard_map/ppermute | solution.py:21
  277.6 22.3 %copy-start.3 = (bf16[4,8,10,384]{3,2,1,0:T(8,128)(2,1)S(1)}, bf16[4,8,10,384]{3,2,1,0:T(8,128)(2,1)}, u32[]{:S(2)}) copy-start(bf16[4,8,10,384]{3,2,1,0:T(8,128)(2,1)} %get-tuple-element.15) | copy-start | bytes 737284
  277.6 22.5 %copy-start.2 = (bf16[4,8,10,384]{3,2,1,0:T(8,128)(2,1)S(1)}, bf16[4,8,10,384]{3,2,1,0:T(8,128)(2,1)}, u32[]{:S(2)}) copy-start(bf16[4,8,10,384]{3,2,1,0:T(8,128)(2,1)} %get-tuple-element.14) | copy-start | bytes 737284
  299.9 13.8 %copy-start.30 = (bf16[320,384]{1,0:T(8,128)(2,1)S(1)}, bf16[320,384]{1,0:T(8,128)(2,1)}, u32[]{:S(2)}) copy-start(bf16[320,384]{1,0:T(8,128)(2,1)} %reshape.234) | copy-start | bytes 737284
  300.1 15.0 %copy-start.13 = (bf16[320,384]{1,0:T(8,128)(2,1)S(1)}, bf16[320,384]{1,0:T(8,128)(2,1)}, u32[]{:S(2)}) copy-start(bf16[320,384]{1,0:T(8,128)(2,1)} %reshape.235) | copy-start | bytes 737284
  300.3 16.1 %slice-start = ((s8[7962624]{0:T(1024)(128)(4,1)}), s8[4194304]{0:T(1024)(128)(4,1)S(1)}, s32[]{:S(2)}) async-start(s8[7962624]{0:T(1024)(128)(4,1)} %bitcast.217), calls=%async_computation.4 | async-start | bytes 8388608
  300.3 16.1 %copy-start.28 = (bf16[320,384]{1,0:T(8,128)(2,1)S(1)}, bf16[320,384]{1,0:T(8,128)(2,1)}, u32[]{:S(2)}) copy-start(bf16[320,384]{1,0:T(8,128)(2,1)} %reshape.236) | copy-start | bytes 737284
  303.3 13.4 %copy-start.27 = (bf16[320,384]{1,0:T(8,128)(2,1)S(1)}, bf16[320,384]{1,0:T(8,128)(2,1)}, u32[]{:S(2)}) copy-start(bf16[320,384]{1,0:T(8,128)(2,1)} %reshape.237) | copy-start | bytes 737284
  304.8 12.3 %copy-start.32 = (bf16[320,384]{1,0:T(8,128)(2,1)S(1)}, bf16[320,384]{1,0:T(8,128)(2,1)}, u32[]{:S(2)}) copy-start(bf16[320,384]{1,0:T(8,128)(2,1)} %reshape.238) | copy-start | bytes 737284
  306.2 11.2 %copy-start.24 = (bf16[320,384]{1,0:T(8,128)(2,1)S(1)}, bf16[320,384]{1,0:T(8,128)(2,1)}, u32[]{:S(2)}) copy-start(bf16[320,384]{1,0:T(8,128)(2,1)} %reshape.240) | copy-start | bytes 737284
  307.7 8.7 %slice-start.1 = ((s8[7962624]{0:T(1024)(128)(4,1)}), s8[3768320]{0:T(1024)(128)(4,1)S(1)}, s32[]{:S(2)}) async-start(s8[7962624]{0:T(1024)(128)(4,1)} %bitcast.217), calls=%async_computation.5 | async-start | bytes 7536640
  307.7 10.1 %copy-start.11 = (bf16[320,384]{1,0:T(8,128)(2,1)S(1)}, bf16[320,384]{1,0:T(8,128)(2,1)}, u32[]{:S(2)}) copy-start(bf16[320,384]{1,0:T(8,128)(2,1)} %reshape.241) | copy-start | bytes 737284
  309.3 8.9 %copy-start.22 = (bf16[320,384]{1,0:T(8,128)(2,1)S(1)}, bf16[320,384]{1,0:T(8,128)(2,1)}, u32[]{:S(2)}) copy-start(bf16[320,384]{1,0:T(8,128)(2,1)} %reshape.242) | copy-start | bytes 737284
  310.8 7.7 %copy-start.21 = (bf16[320,384]{1,0:T(8,128)(2,1)S(1)}, bf16[320,384]{1,0:T(8,128)(2,1)}, u32[]{:S(2)}) copy-start(bf16[320,384]{1,0:T(8,128)(2,1)} %reshape.243) | copy-start | bytes 737284
  312.2 6.6 %copy-start.9 = (bf16[320,384]{1,0:T(8,128)(2,1)S(1)}, bf16[320,384]{1,0:T(8,128)(2,1)}, u32[]{:S(2)}) copy-start(bf16[320,384]{1,0:T(8,128)(2,1)} %reshape.244) | copy-start | bytes 737284
  313.7 5.5 %copy-start.19 = (bf16[320,384]{1,0:T(8,128)(2,1)S(1)}, bf16[320,384]{1,0:T(8,128)(2,1)}, u32[]{:S(2)}) copy-start(bf16[320,384]{1,0:T(8,128)(2,1)} %reshape.245) | copy-start | bytes 737284
  317.8 3.3 copy-start.6
  318.5 3.3 %copy-start.37 = (f32[384]{0:T(512)S(1)}, f32[384]{0:T(512)}, u32[]{:S(2)}) copy-start(f32[384]{0:T(512)} %param.13) | copy-start | bytes 4612
Sparse Core Ops, SparseCore 0:
  9.2 44.1 all-gather.4
  55.2 38.3 all-gather.8
  95.4 80.7 all-gather.6
  177.9 84.2 all-gather.10
where the time goes:
time: 331 us; the launch traced here: 329 us
  waiting for transfers between devices  159 us (48%)
  local copies, waits for them, and re-layouts  79.1 us (24%)
  matrix products  39.5 us (12%)
  starting transfers between devices  32 us (10%)
  between operations  14.3 us (4%)
  other arithmetic  5.48 us (2%)
    all_gather x2, waiting for transfers between devices, convolve(): row_kernel = lax.all_gather(kernel, 'width', axis=1, tiled=True)  81.8 us
    all_gather x2, waiting for transfers between devices, convolve(): lax.all_gather(row_kernel, 'height', axis=1, tiled=True)  66.6 us
    reshape x53, local copies, waits for them, and re-layouts, fold_piece(): window.reshape(-1, count_in)  63 us
    dot_general x54, matrix products, fold_piece(): jnp.dot(window.reshape(-1, count_in), piece[9 * step_t + 3 * step_h + ste...  39.5 us
    ppermute x4, starting transfers between devices, extended(): before = lax.ppermute(last, axis, up)  18.9 us
    slice x6, local copies, waits for them, and re-layouts, fold_piece(): widened[step_t:step_t + frames, step_h:step_h + rows, step_w:step_w + cols]  7.5 us
    all_gather x2, local copies, waits for them, and re-layouts, convolve(): row_kernel = lax.all_gather(kernel, 'width', axis=1, tiled=True)  7.38 us
    ppermute x2, waiting for transfers between devices, passed_along(): return lax.ppermute(x, axis, pairs)  6.76 us
  transfers between devices with their start and end apart: 14, of which 8 were waited for; matrix products, arithmetic and copies ran while one was open for 22% of the time, Pallas kernels for 0%

commit v1 on v0

--- a/solution.py
+++ b/solution.py
@@ -2,6 +2,21 @@
 import jax.numpy as jnp
 from jax import lax
 from jax.sharding import PartitionSpec as P
+from jax.lax import axis_index, axis_size, ppermute
+
+
+def update_fields(payload):
+    ax_name = "width"
+    n_dev_all = axis_size(ax_name)
+    queue = [(to_i, (to_i + 1) % n_dev_all) for to_i in range(n_dev_all)]
+    arr_now = [None] * n_dev_all
+    arr_now[n_dev_all - 1] = payload
+    for dev_i in range(n_dev_all - 2, -1, -1):
+        arr_now[dev_i] = ppermute(arr_now[dev_i + 1], axis_name=ax_name, perm=queue)
+    local_out = jnp.concatenate(arr_now, 1)
+    opened = (axis_index(ax_name) + 1) * payload.shape[1]
+    heard = jnp.roll(local_out, opened, 1)
+    return heard
 
 
 def passed_along(x, axis, by):
@@ -54,7 +69,7 @@
     out_chans = kernel.shape[2]
     empty = jnp.zeros((frames * rows * cols, out_chans), jnp.float32)
     fold_piece = make_folder(widened, frames, rows, cols)
-    row_kernel = lax.all_gather(kernel, "width", axis=1, tiled=True)
+    row_kernel = update_fields(kernel)
     total = fold_piece(
         empty, lax.all_gather(row_kernel, "height", axis=1, tiled=True), jnp.int32(0)
     )

time: 331 us -> 412 us (1.24)
  local copies, waits for them, and re-layouts: 79.1 us -> 118 us
  waiting for transfers between devices: 159 us -> 178 us
  starting transfers between devices: 32 us -> 42.4 us
  other arithmetic: 5.48 us -> 12.1 us
    ppermute x0 -> x30, waiting for transfers between devices: none -> 169 us  [update_fields(): arr_now[dev_i] = ppermute(arr_now[dev_i + 1], axis_name=ax_name, perm=queue)]
    all_gather x2 -> x0, waiting for transfers between devices: 81.8 us -> none  [convolve(): row_kernel = lax.all_gather(kernel, 'width', axis=1, tiled=True)]
    all_gather x2, waiting for transfers between devices: 66.6 us -> 0.02 us  [convolve(): lax.all_gather(row_kernel, 'height', axis=1, tiled=True)]
    concatenate x0 -> x2, local copies, waits for them, and re-layouts: none -> 42.4 us  [update_fields(): local_out = jnp.concatenate(arr_now, 1)]
    ppermute x4, starting transfers between devices: 6.61 us -> 16.7 us  [extended(): after = lax.ppermute(first, axis, down)]
    ppermute x4, starting transfers between devices: 18.9 us -> 10.2 us  [extended(): before = lax.ppermute(last, axis, up)]
    ppermute x0 -> x30, starting transfers between devices: none -> 8.08 us  [update_fields(): arr_now[dev_i] = ppermute(arr_now[dev_i + 1], axis_name=ax_name, perm=queue)]
    unnamed x80 -> x102, local copies, waits for them, and re-layouts: 0.17 us -> 7.76 us
  transfers between devices with their start and end apart: 14 -> 42, of which waited for: 8 -> 34; matrix products, arithmetic and copies ran while one was open for 22% -> 22% of each run, Pallas kernels for 0% -> 0%
where the time goes in v1:
time: 412 us; the launch traced here: 408 us
  waiting for transfers between devices  178 us (43%)
  local copies, waits for them, and re-layouts  118 us (29%)
  starting transfers between devices  42.4 us (10%)
  matrix products  42 us (10%)
  between operations  14.7 us (4%)
  other arithmetic  12.1 us (3%)
    ppermute x30, waiting for transfers between devices, update_fields(): arr_now[dev_i] = ppermute(arr_now[dev_i + 1], axis_name=ax_name, perm=queue)  169 us
    reshape x53, local copies, waits for them, and re-layouts, fold_piece(): window.reshape(-1, count_in)  59.4 us
    concatenate x2, local copies, waits for them, and re-layouts, update_fields(): local_out = jnp.concatenate(arr_now, 1)  42.4 us
    dot_general x54, matrix products, fold_piece(): jnp.dot(window.reshape(-1, count_in), piece[9 * step_t + 3 * step_h + ste...  42 us
    ppermute x4, starting transfers between devices, extended(): after = lax.ppermute(first, axis, down)  16.7 us
    ppermute x4, starting transfers between devices, extended(): before = lax.ppermute(last, axis, up)  10.2 us
  transfers between devices with their start and end apart: 42, of which 34 were waited for; matrix products, arithmetic and copies ran while one was open for 22% of the time, Pallas kernels for 0%

profile of v1, /device:TPU:1, one launch (start us, length us, event | category | flops | bytes accessed | tf_op | source)
XLA Modules:
  0.0 407.6 jit_solution(12340169946971443130)
XLA Ops:
  7.5 3.0 collective-permute-start.4
  10.5 2.3 collective-permute-done.4
  12.8 2.5 collective-permute-start.5
  15.3 2.9 collective-permute-done.5
  18.2 1.8 collective-permute-start.6
  20.1 4.1 %collective-permute-done.6 = bf16[27,6,384]{2,1,0:T(8,128)(2,1)S(1)} collective-permute-done((bf16[27,6,384]{2,1,0:T(8,128)(2,1)S(1)}, bf16[27,6,384]{2,1,0:T(8,128)(2,1)S(1)}, u32[]{:S(2)}, u32[]{:S(2)}) %collective-permute-start.6) | collective-permute-done | bytes 124448 | tf_op jit(solution)/shard_map/ppermute | solution.py:15
  24.8 5.3 %collective-permute-done.7 = bf16[27,6,384]{2,1,0:T(8,128)(2,1)S(1)} collective-permute-done((bf16[27,6,384]{2,1,0:T(8,128)(2,1)S(1)}, bf16[27,6,384]{2,1,0:T(8,128)(2,1)S(1)}, u32[]{:S(2)}, u32[]{:S(2)}) %collective-permute-start.7) | collective-permute-done | bytes 124448 | tf_op jit(solution)/shard_map/ppermute | solution.py:15
  30.2 6.0 %collective-permute-done.8 = bf16[27,6,384]{2,1,0:T(8,128)(2,1)S(1)} collective-permute-done((bf16[27,6,384]{2,1,0:T(8,128)(2,1)S(1)}, bf16[27,6,384]{2,1,0:T(8,128)(2,1)S(1)}, u32[]{:S(2)}, u32[]{:S(2)}) %collective-permute-start.8) | collective-permute-done | bytes 124448 | tf_op jit(solution)/shard_map/ppermute | solution.py:15
  36.2 6.0 %collective-permute-done.9 = bf16[27,6,384]{2,1,0:T(8,128)(2,1)S(1)} collective-permute-done((bf16[27,6,384]{2,1,0:T(8,128)(2,1)S(1)}, bf16[27,6,384]{2,1,0:T(8,128)(2,1)S(1)}, u32[]{:S(2)}, u32[]{:S(2)}) %collective-permute-start.9) | collective-permute-done | bytes 124448 | tf_op jit(solution)/shard_map/ppermute | solution.py:15
  42.1 6.0 %collective-permute-done.10 = bf16[27,6,384]{2,1,0:T(8,128)(2,1)S(1)} collective-permute-done((bf16[27,6,384]{2,1,0:T(8,128)(2,1)S(1)}, bf16[27,6,384]{2,1,0:T(8,128)(2,1)S(1)}, u32[]{:S(2)}, u32[]{:S(2)}) %collective-permute-start.10) | collective-permute-done | bytes 124448 | tf_op jit(solution)/shard_map/ppermute | solution.py:15
  48.1 6.0 %collective-permute-done.11 = bf16[27,6,384]{2,1,0:T(8,128)(2,1)S(1)} collective-permute-done((bf16[27,6,384]{2,1,0:T(8,128)(2,1)S(1)}, bf16[27,6,384]{2,1,0:T(8,128)(2,1)S(1)}, u32[]{:S(2)}, u32[]{:S(2)}) %collective-permute-start.11) | collective-permute-done | bytes 124448 | tf_op jit(solution)/shard_map/ppermute | solution.py:15
  54.8 6.0 %collective-permute-done.12 = bf16[27,6,384]{2,1,0:T(8,128)(2,1)S(1)} collective-permute-done((bf16[27,6,384]{2,1,0:T(8,128)(2,1)S(1)}, bf16[27,6,384]{2,1,0:T(8,128)(2,1)S(1)}, u32[]{:S(2)}, u32[]{:S(2)}) %collective-permute-start.12) | collective-permute-done | bytes 124448 | tf_op jit(solution)/shard_map/ppermute | solution.py:15
  61.4 6.0 %collective-permute-done.13 = bf16[27,6,384]{2,1,0:T(8,128)(2,1)S(1)} collective-permute-done((bf16[27,6,384]{2,1,0:T(8,128)(2,1)S(1)}, bf16[27,6,384]{2,1,0:T(8,128)(2,1)S(1)}, u32[]{:S(2)}, u32[]{:S(2)}) %collective-permute-start.13) | collective-permute-done | bytes 124448 | tf_op jit(solution)/shard_map/ppermute | solution.py:15
  68.0 6.0 %collective-permute-done.14 = bf16[27,6,384]{2,1,0:T(8,128)(2,1)S(1)} collective-permute-done((bf16[27,6,384]{2,1,0:T(8,128)(2,1)S(1)}, bf16[27,6,384]{2,1,0:T(8,128)(2,1)S(1)}, u32[]{:S(2)}, u32[]{:S(2)}) %collective-permute-start.14) | collective-permute-done | bytes 124448 | tf_op jit(solution)/shard_map/ppermute | solution.py:15
  74.7 6.0 %collective-permute-done.15 = bf16[27,6,384]{2,1,0:T(8,128)(2,1)S(1)} collective-permute-done((bf16[27,6,384]{2,1,0:T(8,128)(2,1)S(1)}, bf16[27,6,384]{2,1,0:T(8,128)(2,1)S(1)}, u32[]{:S(2)}, u32[]{:S(2)}) %collective-permute-start.15) | collective-permute-done | bytes 124448 | tf_op jit(solution)/shard_map/ppermute | solution.py:15
  81.3 6.0 %collective-permute-done.16 = bf16[27,6,384]{2,1,0:T(8,128)(2,1)S(1)} collective-permute-done((bf16[27,6,384]{2,1,0:T(8,128)(2,1)S(1)}, bf16[27,6,384]{2,1,0:T(8,128)(2,1)S(1)}, u32[]{:S(2)}, u32[]{:S(2)}) %collective-permute-start.16) | collective-permute-done | bytes 124448 | tf_op jit(solution)/shard_map/ppermute | solution.py:15
  88.0 6.0 %collective-permute-done.17 = bf16[27,6,384]{2,1,0:T(8,128)(2,1)S(1)} collective-permute-done((bf16[27,6,384]{2,1,0:T(8,128)(2,1)S(1)}, bf16[27,6,384]{2,1,0:T(8,128)(2,1)S(1)}, u32[]{:S(2)}, u32[]{:S(2)}) %collective-permute-start.17) | collective-permute-done | bytes 124448 | tf_op jit(solution)/shard_map/ppermute | solution.py:15
  94.6 5.4 %collective-permute-done.18 = bf16[27,6,384]{2,1,0:T(8,128)(2,1)} collective-permute-done((bf16[27,6,384]{2,1,0:T(8,128)(2,1)S(1)}, bf16[27,6,384]{2,1,0:T(8,128)(2,1)}, u32[]{:S(2)}, u32[]{:S(2)}) %collective-permute-start.18) | collective-permute-done | bytes 124448 | tf_op jit(solution)/shard_map/ppermute | solution.py:15
  100.1 20.9 %concatenate.90 = bf16[27,96,384]{2,1,0:T(8,128)(2,1)S(1)} concatenate(bf16[27,6,384]{2,1,0:T(8,128)(2,1)} %collective-permute-done.18, bf16[27,6,384]{2,1,0:T(8,128)(2,1)} %copy-done.37, bf16[27,6,384]{2,1,0:T(8,128)(2,1)} %copy-done.35, bf16[27,6,384]{2,1,0:T(8,128)(2,1)} %copy-done.33, bf16[27,6,384]{2,1,0:T(8,128)(2,1)} %copy-done.32, bf16[27,6,384]{2,1,0:T(8,128)(2,1)} %copy-done.31, ...), dimensions={1} | concatenate | bytes 3981312 | tf_op jit(solution)/shard_map/concatenate | solution.py:16
  120.9 2.8 fusion.1
  124.9 5.9 %collective-permute-done.24 = bf16[27,6,384]{2,1,0:T(8,128)(2,1)S(1)} collective-permute-done((bf16[27,6,384]{2,1,0:T(8,128)(2,1)S(1)}, bf16[27,6,384]{2,1,0:T(8,128)(2,1)S(1)}, u32[]{:S(2)}, u32[]{:S(2)}) %collective-permute-start.24) | collective-permute-done | bytes 124448 | tf_op jit(solution)/shard_map/ppermute | solution.py:15
  130.8 6.0 %collective-permute-done.25 = bf16[27,6,384]{2,1,0:T(8,128)(2,1)S(1)} collective-permute-done((bf16[27,6,384]{2,1,0:T(8,128)(2,1)S(1)}, bf16[27,6,384]{2,1,0:T(8,128)(2,1)S(1)}, u32[]{:S(2)}, u32[]{:S(2)}) %collective-permute-start.25) | collective-permute-done | bytes 124448 | tf_op jit(solution)/shard_map/ppermute | solution.py:15
  136.8 6.0 %collective-permute-done.26 = bf16[27,6,384]{2,1,0:T(8,128)(2,1)S(1)} collective-permute-done((bf16[27,6,384]{2,1,0:T(8,128)(2,1)S(1)}, bf16[27,6,384]{2,1,0:T(8,128)(2,1)S(1)}, u32[]{:S(2)}, u32[]{:S(2)}) %collective-permute-start.26) | collective-permute-done | bytes 124448 | tf_op jit(solution)/shard_map/ppermute | solution.py:15
  142.8 6.0 %collective-permute-done.27 = bf16[27,6,384]{2,1,0:T(8,128)(2,1)S(1)} collective-permute-done((bf16[27,6,384]{2,1,0:T(8,128)(2,1)S(1)}, bf16[27,6,384]{2,1,0:T(8,128)(2,1)S(1)}, u32[]{:S(2)}, u32[]{:S(2)}) %collective-permute-start.27) | collective-permute-done | bytes 124448 | tf_op jit(solution)/shard_map/ppermute | solution.py:15
  148.7 6.0 %collective-permute-done.28 = bf16[27,6,384]{2,1,0:T(8,128)(2,1)S(1)} collective-permute-done((bf16[27,6,384]{2,1,0:T(8,128)(2,1)S(1)}, bf16[27,6,384]{2,1,0:T(8,128)(2,1)S(1)}, u32[]{:S(2)}, u32[]{:S(2)}) %collective-permute-start.28) | collective-permute-done | bytes 124448 | tf_op jit(solution)/shard_map/ppermute | solution.py:15
  154.7 6.0 %collective-permute-done.29 = bf16[27,6,384]{2,1,0:T(8,128)(2,1)S(1)} collective-permute-done((bf16[27,6,384]{2,1,0:T(8,128)(2,1)S(1)}, bf16[27,6,384]{2,1,0:T(8,128)(2,1)S(1)}, u32[]{:S(2)}, u32[]{:S(2)}) %collective-permute-start.29) | collective-permute-done | bytes 124448 | tf_op jit(solution)/shard_map/ppermute | solution.py:15
  160.7 6.0 %collective-permute-done.30 = bf16[27,6,384]{2,1,0:T(8,128)(2,1)S(1)} collective-permute-done((bf16[27,6,384]{2,1,0:T(8,128)(2,1)S(1)}, bf16[27,6,384]{2,1,0:T(8,128)(2,1)S(1)}, u32[]{:S(2)}, u32[]{:S(2)}) %collective-permute-start.30) | collective-permute-done | bytes 124448 | tf_op jit(solution)/shard_map/ppermute | solution.py:15
  166.7 6.0 %collective-permute-done.31 = bf16[27,6,384]{2,1,0:T(8,128)(2,1)S(1)} collective-permute-done((bf16[27,6,384]{2,1,0:T(8,128)(2,1)S(1)}, bf16[27,6,384]{2,1,0:T(8,128)(2,1)S(1)}, u32[]{:S(2)}, u32[]{:S(2)}) %collective-permute-start.31) | collective-permute-done | bytes 124448 | tf_op jit(solution)/shard_map/ppermute | solution.py:15
  172.6 6.0 %collective-permute-done.32 = bf16[27,6,384]{2,1,0:T(8,128)(2,1)S(1)} collective-permute-done((bf16[27,6,384]{2,1,0:T(8,128)(2,1)S(1)}, bf16[27,6,384]{2,1,0:T(8,128)(2,1)S(1)}, u32[]{:S(2)}, u32[]{:S(2)}) %collective-permute-start.32) | collective-permute-done | bytes 124448 | tf_op jit(solution)/shard_map/ppermute | solution.py:15
  178.6 6.0 %collective-permute-done.33 = bf16[27,6,384]{2,1,0:T(8,128)(2,1)S(1)} collective-permute-done((bf16[27,6,384]{2,1,0:T(8,128)(2,1)S(1)}, bf16[27,6,384]{2,1,0:T(8,128)(2,1)S(1)}, u32[]{:S(2)}, u32[]{:S(2)}) %collective-permute-start.33) | collective-permute-done | bytes 124448 | tf_op jit(solution)/shard_map/ppermute | solution.py:15
  184.6 6.0 %collective-permute-done.34 = bf16[27,6,384]{2,1,0:T(8,128)(2,1)S(1)} collective-permute-done((bf16[27,6,384]{2,1,0:T(8,128)(2,1)S(1)}, bf16[27,6,384]{2,1,0:T(8,128)(2,1)S(1)}, u32[]{:S(2)}, u32[]{:S(2)}) %collective-permute-start.34) | collective-permute-done | bytes 124448 | tf_op jit(solution)/shard_map/ppermute | solution.py:15
  190.6 6.0 %collective-permute-done.35 = bf16[27,6,384]{2,1,0:T(8,128)(2,1)S(1)} collective-permute-done((bf16[27,6,384]{2,1,0:T(8,128)(2,1)S(1)}, bf16[27,6,384]{2,1,0:T(8,128)(2,1)S(1)}, u32[]{:S(2)}, u32[]{:S(2)}) %collective-permute-start.35) | collective-permute-done | bytes 124448 | tf_op jit(solution)/shard_map/ppermute | solution.py:15
  196.6 6.0 %collective-permute-done.36 = bf16[27,6,384]{2,1,0:T(8,128)(2,1)S(1)} collective-permute-done((bf16[27,6,384]{2,1,0:T(8,128)(2,1)S(1)}, bf16[27,6,384]{2,1,0:T(8,128)(2,1)S(1)}, u32[]{:S(2)}, u32[]{:S(2)}) %collective-permute-start.36) | collective-permute-done | bytes 124448 | tf_op jit(solution)/shard_map/ppermute | solution.py:15
  202.5 6.0 %collective-permute-done.37 = bf16[27,6,384]{2,1,0:T(8,128)(2,1)S(1)} collective-permute-done((bf16[27,6,384]{2,1,0:T(8,128)(2,1)S(1)}, bf16[27,6,384]{2,1,0:T(8,128)(2,1)S(1)}, u32[]{:S(2)}, u32[]{:S(2)}) %collective-permute-start.37) | collective-permute-done | bytes 124448 | tf_op jit(solution)/shard_map/ppermute | solution.py:15
  209.2 5.4 %collective-permute-done.38 = bf16[27,6,384]{2,1,0:T(8,128)(2,1)} collective-permute-done((bf16[27,6,384]{2,1,0:T(8,128)(2,1)S(1)}, bf16[27,6,384]{2,1,0:T(8,128)(2,1)}, u32[]{:S(2)}, u32[]{:S(2)}) %collective-permute-start.38) | collective-permute-done | bytes 124448 | tf_op jit(solution)/shard_map/ppermute | solution.py:15
  214.6 21.5 %concatenate.97 = bf16[27,96,384]{2,1,0:T(8,128)(2,1)S(1)} concatenate(bf16[27,6,384]{2,1,0:T(8,128)(2,1)} %collective-permute-done.38, bf16[27,6,384]{2,1,0:T(8,128)(2,1)} %copy-done.43, bf16[27,6,384]{2,1,0:T(8,128)(2,1)} %copy-done.42, bf16[27,6,384]{2,1,0:T(8,128)(2,1)} %copy-done.41, bf16[27,6,384]{2,1,0:T(8,128)(2,1)} %copy-done.40, bf16[27,6,384]{2,1,0:T(8,128)(2,1)} %copy-done.39, ...), dimensions={1} | concatenate | bytes 3981312 | tf_op jit(solution)/shard_map/concatenate | solution.py:16
  236.1 2.9 fusion
  239.6 3.2 collective-permute-start
  245.4 3.1 collective-permute-start.1
  251.6 2.1 collective-permute-done.2
  254.5 9.2 %collective-permute-start.19 = (bf16[6,10,1,384]{3,2,1,0:T(2,128)(2,1)}, bf16[6,10,1,384]{3,2,1,0:T(2,128)(2,1)S(1)}, u32[]{:S(2)}, u32[]{:S(2)}) collective-permute-start(bf16[6,10,1,384]{3,2,1,0:T(2,128)(2,1)} %get-tuple-element.49), channel_id=1, source_target_pairs={{1,0},{2,1},{3,2},{4,3},{5,4},{6,5},{7,6},{8,7},{9,8},{10,9},{11,1... | collective-permute-start | bytes 138248 | tf_op jit(solution)/shard_map/ppermute | solution.py:36
  263.7 2.1 collective-permute-start.3
  271.8 2.3 fusion.34
  274.1 1.8 reshape.197
  275.9 1.8 reshape.199
  277.7 1.8 reshape.200
  281.2 1.8 reshape.203
  284.8 1.8 reshape.206
  288.4 1.8 reshape.209
  295.8 2.2 fusion.25
  314.7 4.1 %collective-permute-start.20 = (bf16[2,8,10,384]{3,2,1,0:T(8,128)(2,1)S(1)}, bf16[2,8,10,384]{3,2,1,0:T(8,128)(2,1)S(1)}, u32[]{:S(2)}, u32[]{:S(2)}) collective-permute-start(bf16[2,8,10,384]{3,2,1,0:T(8,128)(2,1)S(1)} %slice.566), channel_id=1, source_target_pairs={{0,64},{64,128},{128,192},{1,65},{65,129},{129,193},{2,66},{66,130... | collective-permute-start | bytes 368648 | tf_op jit(solution)/shard_map/ppermute | solution.py:25
  318.8 3.7 collective-permute-done.20
  322.6 3.1 collective-permute-start.21
  328.9 1.9 collective-permute-done.22
  333.2 1.9 collective-permute-start.23
  335.2 4.7 %collective-permute-start.39 = (bf16[6,10,1,384]{3,2,1,0:T(2,128)(2,1)}, bf16[6,10,1,384]{3,2,1,0:T(2,128)(2,1)}, u32[]{:S(2)}, u32[]{:S(2)}) collective-permute-start(bf16[6,10,1,384]{3,2,1,0:T(2,128)(2,1)} %get-tuple-element.27), channel_id=1, source_target_pairs={{1,0},{2,1},{3,2},{4,3},{5,4},{6,5},{7,6},{8,7},{9,8},{10,9},{11,1... | collective-permute-start | bytes 138248 | tf_op jit(solution)/shard_map/ppermute | solution.py:36
  344.8 1.8 reshape.241
  347.4 1.8 reshape.249
  352.4 1.8 reshape.225
  354.2 2.0 fusion.32
  356.3 1.9 reshape.227
  358.1 1.8 reshape.228
  363.5 1.8 reshape.233
  368.8 1.8 reshape.237
  (264 shorter events, 99.5 us)
Async XLA Ops:
  6.5 287.6 %all-gather.3.cloned.1.call-start = ((), (), s32[]{:S(2)}) async-start(), calls=%async_computation | async-start | bytes 9953280 | tf_op jit(solution)/shard_map/all_gather | solution.py:74
  7.5 5.3 %collective-permute-start.4 = (bf16[27,6,384]{2,1,0:T(8,128)(2,1)S(1)}, bf16[27,6,384]{2,1,0:T(8,128)(2,1)S(1)}, u32[]{:S(2)}, u32[]{:S(2)}) collective-permute-start(bf16[27,6,384]{2,1,0:T(8,128)(2,1)S(1)} %copy.11), channel_id=1, source_target_pairs={{0,1},{1,2},{2,3},{3,4},{4,5},{5,6},{6,7},{7,8},{8,9},{9,10},{10,1... | collective-permute-start | bytes 373256 | tf_op jit(solution)/shard_map/ppermute | solution.py:15
  12.8 5.4 %collective-permute-start.5 = (bf16[27,6,384]{2,1,0:T(8,128)(2,1)S(1)}, bf16[27,6,384]{2,1,0:T(8,128)(2,1)S(1)}, u32[]{:S(2)}, u32[]{:S(2)}) collective-permute-start(bf16[27,6,384]{2,1,0:T(8,128)(2,1)S(1)} %collective-permute-done.4), channel_id=1, source_target_pairs={{0,1},{1,2},{2,3},{3,4},{4,5},{5,6},{6,7},{7,8},{8,9},{9,10},{10,1... | collective-permute-start | bytes 373256 | tf_op jit(solution)/shard_map/ppermute | solution.py:15
  18.2 6.0 %collective-permute-start.6 = (bf16[27,6,384]{2,1,0:T(8,128)(2,1)S(1)}, bf16[27,6,384]{2,1,0:T(8,128)(2,1)S(1)}, u32[]{:S(2)}, u32[]{:S(2)}) collective-permute-start(bf16[27,6,384]{2,1,0:T(8,128)(2,1)S(1)} %collective-permute-done.5), channel_id=1, source_target_pairs={{0,1},{1,2},{2,3},{3,4},{4,5},{5,6},{6,7},{7,8},{8,9},{9,10},{10,1... | collective-permute-start | bytes 373256 | tf_op jit(solution)/shard_map/ppermute | solution.py:15
  24.2 6.0 %collective-permute-start.7 = (bf16[27,6,384]{2,1,0:T(8,128)(2,1)S(1)}, bf16[27,6,384]{2,1,0:T(8,128)(2,1)S(1)}, u32[]{:S(2)}, u32[]{:S(2)}) collective-permute-start(bf16[27,6,384]{2,1,0:T(8,128)(2,1)S(1)} %collective-permute-done.6), channel_id=1, source_target_pairs={{0,1},{1,2},{2,3},{3,4},{4,5},{5,6},{6,7},{7,8},{8,9},{9,10},{10,1... | collective-permute-start | bytes 373256 | tf_op jit(solution)/shard_map/ppermute | solution.py:15
  30.2 6.0 %collective-permute-start.8 = (bf16[27,6,384]{2,1,0:T(8,128)(2,1)S(1)}, bf16[27,6,384]{2,1,0:T(8,128)(2,1)S(1)}, u32[]{:S(2)}, u32[]{:S(2)}) collective-permute-start(bf16[27,6,384]{2,1,0:T(8,128)(2,1)S(1)} %collective-permute-done.7), channel_id=1, source_target_pairs={{0,1},{1,2},{2,3},{3,4},{4,5},{5,6},{6,7},{7,8},{8,9},{9,10},{10,1... | collective-permute-start | bytes 373256 | tf_op jit(solution)/shard_map/ppermute | solution.py:15
  36.2 6.0 %collective-permute-start.9 = (bf16[27,6,384]{2,1,0:T(8,128)(2,1)S(1)}, bf16[27,6,384]{2,1,0:T(8,128)(2,1)S(1)}, u32[]{:S(2)}, u32[]{:S(2)}) collective-permute-start(bf16[27,6,384]{2,1,0:T(8,128)(2,1)S(1)} %collective-permute-done.8), channel_id=1, source_target_pairs={{0,1},{1,2},{2,3},{3,4},{4,5},{5,6},{6,7},{7,8},{8,9},{9,10},{10,1... | collective-permute-start | bytes 373256 | tf_op jit(solution)/shard_map/ppermute | solution.py:15
  42.1 6.0 %collective-permute-start.10 = (bf16[27,6,384]{2,1,0:T(8,128)(2,1)S(1)}, bf16[27,6,384]{2,1,0:T(8,128)(2,1)S(1)}, u32[]{:S(2)}, u32[]{:S(2)}) collective-permute-start(bf16[27,6,384]{2,1,0:T(8,128)(2,1)S(1)} %collective-permute-done.9), channel_id=1, source_target_pairs={{0,1},{1,2},{2,3},{3,4},{4,5},{5,6},{6,7},{7,8},{8,9},{9,10},{10,1... | collective-permute-start | bytes 373256 | tf_op jit(solution)/shard_map/ppermute | solution.py:15
  48.1 6.0 %collective-permute-start.11 = (bf16[27,6,384]{2,1,0:T(8,128)(2,1)S(1)}, bf16[27,6,384]{2,1,0:T(8,128)(2,1)S(1)}, u32[]{:S(2)}, u32[]{:S(2)}) collective-permute-start(bf16[27,6,384]{2,1,0:T(8,128)(2,1)S(1)} %collective-permute-done.10), channel_id=1, source_target_pairs={{0,1},{1,2},{2,3},{3,4},{4,5},{5,6},{6,7},{7,8},{8,9},{9,10},{10,1... | collective-permute-start | bytes 373256 | tf_op jit(solution)/shard_map/ppermute | solution.py:15
  54.8 6.0 %collective-permute-start.12 = (bf16[27,6,384]{2,1,0:T(8,128)(2,1)S(1)}, bf16[27,6,384]{2,1,0:T(8,128)(2,1)S(1)}, u32[]{:S(2)}, u32[]{:S(2)}) collective-permute-start(bf16[27,6,384]{2,1,0:T(8,128)(2,1)S(1)} %collective-permute-done.11), channel_id=1, source_target_pairs={{0,1},{1,2},{2,3},{3,4},{4,5},{5,6},{6,7},{7,8},{8,9},{9,10},{10,1... | collective-permute-start | bytes 373256 | tf_op jit(solution)/shard_map/ppermute | solution.py:15
  61.4 6.0 %collective-permute-start.13 = (bf16[27,6,384]{2,1,0:T(8,128)(2,1)S(1)}, bf16[27,6,384]{2,1,0:T(8,128)(2,1)S(1)}, u32[]{:S(2)}, u32[]{:S(2)}) collective-permute-start(bf16[27,6,384]{2,1,0:T(8,128)(2,1)S(1)} %collective-permute-done.12), channel_id=1, source_target_pairs={{0,1},{1,2},{2,3},{3,4},{4,5},{5,6},{6,7},{7,8},{8,9},{9,10},{10,1... | collective-permute-start | bytes 373256 | tf_op jit(solution)/shard_map/ppermute | solution.py:15
  68.0 6.0 %collective-permute-start.14 = (bf16[27,6,384]{2,1,0:T(8,128)(2,1)S(1)}, bf16[27,6,384]{2,1,0:T(8,128)(2,1)S(1)}, u32[]{:S(2)}, u32[]{:S(2)}) collective-permute-start(bf16[27,6,384]{2,1,0:T(8,128)(2,1)S(1)} %collective-permute-done.13), channel_id=1, source_target_pairs={{0,1},{1,2},{2,3},{3,4},{4,5},{5,6},{6,7},{7,8},{8,9},{9,10},{10,1... | collective-permute-start | bytes 373256 | tf_op jit(solution)/shard_map/ppermute | solution.py:15
  74.7 6.0 %collective-permute-start.15 = (bf16[27,6,384]{2,1,0:T(8,128)(2,1)S(1)}, bf16[27,6,384]{2,1,0:T(8,128)(2,1)S(1)}, u32[]{:S(2)}, u32[]{:S(2)}) collective-permute-start(bf16[27,6,384]{2,1,0:T(8,128)(2,1)S(1)} %collective-permute-done.14), channel_id=1, source_target_pairs={{0,1},{1,2},{2,3},{3,4},{4,5},{5,6},{6,7},{7,8},{8,9},{9,10},{10,1... | collective-permute-start | bytes 373256 | tf_op jit(solution)/shard_map/ppermute | solution.py:15
  81.3 6.0 %collective-permute-start.16 = (bf16[27,6,384]{2,1,0:T(8,128)(2,1)S(1)}, bf16[27,6,384]{2,1,0:T(8,128)(2,1)S(1)}, u32[]{:S(2)}, u32[]{:S(2)}) collective-permute-start(bf16[27,6,384]{2,1,0:T(8,128)(2,1)S(1)} %collective-permute-done.15), channel_id=1, source_target_pairs={{0,1},{1,2},{2,3},{3,4},{4,5},{5,6},{6,7},{7,8},{8,9},{9,10},{10,1... | collective-permute-start | bytes 373256 | tf_op jit(solution)/shard_map/ppermute | solution.py:15
  88.0 6.0 %collective-permute-start.17 = (bf16[27,6,384]{2,1,0:T(8,128)(2,1)S(1)}, bf16[27,6,384]{2,1,0:T(8,128)(2,1)S(1)}, u32[]{:S(2)}, u32[]{:S(2)}) collective-permute-start(bf16[27,6,384]{2,1,0:T(8,128)(2,1)S(1)} %collective-permute-done.16), channel_id=1, source_target_pairs={{0,1},{1,2},{2,3},{3,4},{4,5},{5,6},{6,7},{7,8},{8,9},{9,10},{10,1... | collective-permute-start | bytes 373256 | tf_op jit(solution)/shard_map/ppermute | solution.py:15
  93.9 6.1 %collective-permute-start.18 = (bf16[27,6,384]{2,1,0:T(8,128)(2,1)S(1)}, bf16[27,6,384]{2,1,0:T(8,128)(2,1)}, u32[]{:S(2)}, u32[]{:S(2)}) collective-permute-start(bf16[27,6,384]{2,1,0:T(8,128)(2,1)S(1)} %collective-permute-done.17), channel_id=1, source_target_pairs={{0,1},{1,2},{2,3},{3,4},{4,5},{5,6},{6,7},{7,8},{8,9},{9,10},{10,1... | collective-permute-start | bytes 373256 | tf_op jit(solution)/shard_map/ppermute | solution.py:15
  120.9 118.1 %copy-start.1 = (bf16[4,8,10,384]{3,1,2,0:T(8,128)(2,1)S(1)}, bf16[4,8,10,384]{3,1,2,0:T(8,128)(2,1)}, u32[]{:S(2)}) copy-start(bf16[4,8,10,384]{3,1,2,0:T(8,128)(2,1)} %param.9) | copy-start | bytes 737284
  120.9 118.3 %copy-start.45 = (f32[384]{0:T(512)S(1)}, f32[384]{0:T(512)}, u32[]{:S(2)}) copy-start(f32[384]{0:T(512)} %param.10) | copy-start | bytes 4612
  123.8 217.1 %all-gather.5.cloned.1.call-start = ((), (), s32[]{:S(2)}) async-start(), calls=%async_computation.1 | async-start | bytes 9953280 | tf_op jit(solution)/shard_map/all_gather | solution.py:74
  124.8 6.0 %collective-permute-start.24 = (bf16[27,6,384]{2,1,0:T(8,128)(2,1)S(1)}, bf16[27,6,384]{2,1,0:T(8,128)(2,1)S(1)}, u32[]{:S(2)}, u32[]{:S(2)}) collective-permute-start(bf16[27,6,384]{2,1,0:T(8,128)(2,1)S(1)} %copy.13), channel_id=1, source_target_pairs={{0,1},{1,2},{2,3},{3,4},{4,5},{5,6},{6,7},{7,8},{8,9},{9,10},{10,1... | collective-permute-start | bytes 373256 | tf_op jit(solution)/shard_map/ppermute | solution.py:15
  130.8 6.0 %collective-permute-start.25 = (bf16[27,6,384]{2,1,0:T(8,128)(2,1)S(1)}, bf16[27,6,384]{2,1,0:T(8,128)(2,1)S(1)}, u32[]{:S(2)}, u32[]{:S(2)}) collective-permute-start(bf16[27,6,384]{2,1,0:T(8,128)(2,1)S(1)} %collective-permute-done.24), channel_id=1, source_target_pairs={{0,1},{1,2},{2,3},{3,4},{4,5},{5,6},{6,7},{7,8},{8,9},{9,10},{10,1... | collective-permute-start | bytes 373256 | tf_op jit(solution)/shard_map/ppermute | solution.py:15
  136.8 6.0 %collective-permute-start.26 = (bf16[27,6,384]{2,1,0:T(8,128)(2,1)S(1)}, bf16[27,6,384]{2,1,0:T(8,128)(2,1)S(1)}, u32[]{:S(2)}, u32[]{:S(2)}) collective-permute-start(bf16[27,6,384]{2,1,0:T(8,128)(2,1)S(1)} %collective-permute-done.25), channel_id=1, source_target_pairs={{0,1},{1,2},{2,3},{3,4},{4,5},{5,6},{6,7},{7,8},{8,9},{9,10},{10,1... | collective-permute-start | bytes 373256 | tf_op jit(solution)/shard_map/ppermute | solution.py:15
  142.7 6.0 %collective-permute-start.27 = (bf16[27,6,384]{2,1,0:T(8,128)(2,1)S(1)}, bf16[27,6,384]{2,1,0:T(8,128)(2,1)S(1)}, u32[]{:S(2)}, u32[]{:S(2)}) collective-permute-start(bf16[27,6,384]{2,1,0:T(8,128)(2,1)S(1)} %collective-permute-done.26), channel_id=1, source_target_pairs={{0,1},{1,2},{2,3},{3,4},{4,5},{5,6},{6,7},{7,8},{8,9},{9,10},{10,1... | collective-permute-start | bytes 373256 | tf_op jit(solution)/shard_map/ppermute | solution.py:15
  148.7 6.0 %collective-permute-start.28 = (bf16[27,6,384]{2,1,0:T(8,128)(2,1)S(1)}, bf16[27,6,384]{2,1,0:T(8,128)(2,1)S(1)}, u32[]{:S(2)}, u32[]{:S(2)}) collective-permute-start(bf16[27,6,384]{2,1,0:T(8,128)(2,1)S(1)} %collective-permute-done.27), channel_id=1, source_target_pairs={{0,1},{1,2},{2,3},{3,4},{4,5},{5,6},{6,7},{7,8},{8,9},{9,10},{10,1... | collective-permute-start | bytes 373256 | tf_op jit(solution)/shard_map/ppermute | solution.py:15
  154.7 6.0 %collective-permute-start.29 = (bf16[27,6,384]{2,1,0:T(8,128)(2,1)S(1)}, bf16[27,6,384]{2,1,0:T(8,128)(2,1)S(1)}, u32[]{:S(2)}, u32[]{:S(2)}) collective-permute-start(bf16[27,6,384]{2,1,0:T(8,128)(2,1)S(1)} %collective-permute-done.28), channel_id=1, source_target_pairs={{0,1},{1,2},{2,3},{3,4},{4,5},{5,6},{6,7},{7,8},{8,9},{9,10},{10,1... | collective-permute-start | bytes 373256 | tf_op jit(solution)/shard_map/ppermute | solution.py:15
  160.7 6.0 %collective-permute-start.30 = (bf16[27,6,384]{2,1,0:T(8,128)(2,1)S(1)}, bf16[27,6,384]{2,1,0:T(8,128)(2,1)S(1)}, u32[]{:S(2)}, u32[]{:S(2)}) collective-permute-start(bf16[27,6,384]{2,1,0:T(8,128)(2,1)S(1)} %collective-permute-done.29), channel_id=1, source_target_pairs={{0,1},{1,2},{2,3},{3,4},{4,5},{5,6},{6,7},{7,8},{8,9},{9,10},{10,1... | collective-permute-start | bytes 373256 | tf_op jit(solution)/shard_map/ppermute | solution.py:15
  166.7 41.9 %copy-start.34 = (bf16[27,6,384]{2,1,0:T(8,128)(2,1)}, bf16[27,6,384]{2,1,0:T(8,128)(2,1)S(1)}, u32[]{:S(2)}) copy-start(bf16[27,6,384]{2,1,0:T(8,128)(2,1)S(1)} %collective-permute-done.30) | copy-start | bytes 373252
  166.7 6.0 %collective-permute-start.31 = (bf16[27,6,384]{2,1,0:T(8,128)(2,1)S(1)}, bf16[27,6,384]{2,1,0:T(8,128)(2,1)S(1)}, u32[]{:S(2)}, u32[]{:S(2)}) collective-permute-start(bf16[27,6,384]{2,1,0:T(8,128)(2,1)S(1)} %collective-permute-done.30), channel_id=1, source_target_pairs={{0,1},{1,2},{2,3},{3,4},{4,5},{5,6},{6,7},{7,8},{8,9},{9,10},{10,1... | collective-permute-start | bytes 373256 | tf_op jit(solution)/shard_map/ppermute | solution.py:15
  172.6 35.9 %copy-start.36 = (bf16[27,6,384]{2,1,0:T(8,128)(2,1)}, bf16[27,6,384]{2,1,0:T(8,128)(2,1)S(1)}, u32[]{:S(2)}) copy-start(bf16[27,6,384]{2,1,0:T(8,128)(2,1)S(1)} %collective-permute-done.31) | copy-start | bytes 373252
  172.6 6.0 %collective-permute-start.32 = (bf16[27,6,384]{2,1,0:T(8,128)(2,1)S(1)}, bf16[27,6,384]{2,1,0:T(8,128)(2,1)S(1)}, u32[]{:S(2)}, u32[]{:S(2)}) collective-permute-start(bf16[27,6,384]{2,1,0:T(8,128)(2,1)S(1)} %collective-permute-done.31), channel_id=1, source_target_pairs={{0,1},{1,2},{2,3},{3,4},{4,5},{5,6},{6,7},{7,8},{8,9},{9,10},{10,1... | collective-permute-start | bytes 373256 | tf_op jit(solution)/shard_map/ppermute | solution.py:15
  178.6 29.9 %copy-start.38 = (bf16[27,6,384]{2,1,0:T(8,128)(2,1)}, bf16[27,6,384]{2,1,0:T(8,128)(2,1)S(1)}, u32[]{:S(2)}) copy-start(bf16[27,6,384]{2,1,0:T(8,128)(2,1)S(1)} %collective-permute-done.32) | copy-start | bytes 373252
  178.6 6.0 %collective-permute-start.33 = (bf16[27,6,384]{2,1,0:T(8,128)(2,1)S(1)}, bf16[27,6,384]{2,1,0:T(8,128)(2,1)S(1)}, u32[]{:S(2)}, u32[]{:S(2)}) collective-permute-start(bf16[27,6,384]{2,1,0:T(8,128)(2,1)S(1)} %collective-permute-done.32), channel_id=1, source_target_pairs={{0,1},{1,2},{2,3},{3,4},{4,5},{5,6},{6,7},{7,8},{8,9},{9,10},{10,1... | collective-permute-start | bytes 373256 | tf_op jit(solution)/shard_map/ppermute | solution.py:15
  184.6 24.0 %copy-start.39 = (bf16[27,6,384]{2,1,0:T(8,128)(2,1)}, bf16[27,6,384]{2,1,0:T(8,128)(2,1)S(1)}, u32[]{:S(2)}) copy-start(bf16[27,6,384]{2,1,0:T(8,128)(2,1)S(1)} %collective-permute-done.33) | copy-start | bytes 373252
  184.6 6.0 %collective-permute-start.34 = (bf16[27,6,384]{2,1,0:T(8,128)(2,1)S(1)}, bf16[27,6,384]{2,1,0:T(8,128)(2,1)S(1)}, u32[]{:S(2)}, u32[]{:S(2)}) collective-permute-start(bf16[27,6,384]{2,1,0:T(8,128)(2,1)S(1)} %collective-permute-done.33), channel_id=1, source_target_pairs={{0,1},{1,2},{2,3},{3,4},{4,5},{5,6},{6,7},{7,8},{8,9},{9,10},{10,1... | collective-permute-start | bytes 373256 | tf_op jit(solution)/shard_map/ppermute | solution.py:15
  190.6 18.0 %copy-start.40 = (bf16[27,6,384]{2,1,0:T(8,128)(2,1)}, bf16[27,6,384]{2,1,0:T(8,128)(2,1)S(1)}, u32[]{:S(2)}) copy-start(bf16[27,6,384]{2,1,0:T(8,128)(2,1)S(1)} %collective-permute-done.34) | copy-start | bytes 373252
  190.6 6.0 %collective-permute-start.35 = (bf16[27,6,384]{2,1,0:T(8,128)(2,1)S(1)}, bf16[27,6,384]{2,1,0:T(8,128)(2,1)S(1)}, u32[]{:S(2)}, u32[]{:S(2)}) collective-permute-start(bf16[27,6,384]{2,1,0:T(8,128)(2,1)S(1)} %collective-permute-done.34), channel_id=1, source_target_pairs={{0,1},{1,2},{2,3},{3,4},{4,5},{5,6},{6,7},{7,8},{8,9},{9,10},{10,1... | collective-permute-start | bytes 373256 | tf_op jit(solution)/shard_map/ppermute | solution.py:15
  196.6 12.0 %copy-start.41 = (bf16[27,6,384]{2,1,0:T(8,128)(2,1)}, bf16[27,6,384]{2,1,0:T(8,128)(2,1)S(1)}, u32[]{:S(2)}) copy-start(bf16[27,6,384]{2,1,0:T(8,128)(2,1)S(1)} %collective-permute-done.35) | copy-start | bytes 373252
  196.6 6.0 %collective-permute-start.36 = (bf16[27,6,384]{2,1,0:T(8,128)(2,1)S(1)}, bf16[27,6,384]{2,1,0:T(8,128)(2,1)S(1)}, u32[]{:S(2)}, u32[]{:S(2)}) collective-permute-start(bf16[27,6,384]{2,1,0:T(8,128)(2,1)S(1)} %collective-permute-done.35), channel_id=1, source_target_pairs={{0,1},{1,2},{2,3},{3,4},{4,5},{5,6},{6,7},{7,8},{8,9},{9,10},{10,1... | collective-permute-start | bytes 373256 | tf_op jit(solution)/shard_map/ppermute | solution.py:15
  202.5 6.0 %collective-permute-start.37 = (bf16[27,6,384]{2,1,0:T(8,128)(2,1)S(1)}, bf16[27,6,384]{2,1,0:T(8,128)(2,1)S(1)}, u32[]{:S(2)}, u32[]{:S(2)}) collective-permute-start(bf16[27,6,384]{2,1,0:T(8,128)(2,1)S(1)} %collective-permute-done.36), channel_id=1, source_target_pairs={{0,1},{1,2},{2,3},{3,4},{4,5},{5,6},{6,7},{7,8},{8,9},{9,10},{10,1... | collective-permute-start | bytes 373256 | tf_op jit(solution)/shard_map/ppermute | solution.py:15
  208.5 6.1 %collective-permute-start.38 = (bf16[27,6,384]{2,1,0:T(8,128)(2,1)S(1)}, bf16[27,6,384]{2,1,0:T(8,128)(2,1)}, u32[]{:S(2)}, u32[]{:S(2)}) collective-permute-start(bf16[27,6,384]{2,1,0:T(8,128)(2,1)S(1)} %collective-permute-done.37), channel_id=1, source_target_pairs={{0,1},{1,2},{2,3},{3,4},{4,5},{5,6},{6,7},{7,8},{8,9},{9,10},{10,1... | collective-permute-start | bytes 373256 | tf_op jit(solution)/shard_map/ppermute | solution.py:15
  239.6 5.8 %collective-permute-start = (bf16[2,8,10,384]{3,2,1,0:T(8,128)(2,1)S(1)}, bf16[2,8,10,384]{3,2,1,0:T(8,128)(2,1)S(1)}, u32[]{:S(2)}, u32[]{:S(2)}) collective-permute-start(bf16[2,8,10,384]{3,2,1,0:T(8,128)(2,1)S(1)} %slice.512), channel_id=1, source_target_pairs={{0,64},{64,128},{128,192},{1,65},{65,129},{129,193},{2,66},{66,130... | collective-permute-start | bytes 368648 | tf_op jit(solution)/shard_map/ppermute | solution.py:25
  245.4 6.1 %collective-permute-start.1 = (bf16[6,1,10,384]{3,2,1,0:T(8,128)(2,1)S(1)}, bf16[6,1,10,384]{3,2,1,0:T(8,128)(2,1)S(1)}, u32[]{:S(2)}, u32[]{:S(2)}) collective-permute-start(bf16[6,1,10,384]{3,2,1,0:T(8,128)(2,1)S(1)} %get-tuple-element.72), channel_id=1, source_target_pairs={{0,16},{16,32},{32,48},{1,17},{17,33},{33,49},{2,18},{18,34},{34,5... | collective-permute-start | bytes 138248 | tf_op jit(solution)/shard_map/ppermute | solution.py:35
  248.6 5.1 %collective-permute-start.2 = (bf16[6,1,10,384]{3,2,1,0:T(8,128)(2,1)S(1)}, bf16[6,1,10,384]{3,2,1,0:T(8,128)(2,1)S(1)}, u32[]{:S(2)}, u32[]{:S(2)}) collective-permute-start(bf16[6,1,10,384]{3,2,1,0:T(8,128)(2,1)S(1)} %get-tuple-element.73), channel_id=1, source_target_pairs={{16,0},{32,16},{48,32},{17,1},{33,17},{49,33},{18,2},{34,18},{50,3... | collective-permute-start | bytes 138248 | tf_op jit(solution)/shard_map/ppermute | solution.py:36
  254.5 16.6 %collective-permute-start.19 = (bf16[6,10,1,384]{3,2,1,0:T(2,128)(2,1)}, bf16[6,10,1,384]{3,2,1,0:T(2,128)(2,1)S(1)}, u32[]{:S(2)}, u32[]{:S(2)}) collective-permute-start(bf16[6,10,1,384]{3,2,1,0:T(2,128)(2,1)} %get-tuple-element.49), channel_id=1, source_target_pairs={{1,0},{2,1},{3,2},{4,3},{5,4},{6,5},{7,6},{8,7},{9,8},{10,9},{11,1... | collective-permute-start | bytes 138248 | tf_op jit(solution)/shard_map/ppermute | solution.py:36
  263.7 7.4 %collective-permute-start.3 = (bf16[6,10,1,384]{3,2,1,0:T(2,128)(2,1)}, bf16[6,10,1,384]{3,2,1,0:T(2,128)(2,1)S(1)}, u32[]{:S(2)}, u32[]{:S(2)}) collective-permute-start(bf16[6,10,1,384]{3,2,1,0:T(2,128)(2,1)} %get-tuple-element.48), channel_id=1, source_target_pairs={{0,1},{1,2},{2,3},{3,4},{4,5},{5,6},{6,7},{7,8},{8,9},{9,10},{10,1... | collective-permute-start | bytes 138248 | tf_op jit(solution)/shard_map/ppermute | solution.py:35
  292.7 12.7 %copy-start.14 = (bf16[320,384]{1,0:T(8,128)(2,1)S(1)}, bf16[320,384]{1,0:T(8,128)(2,1)}, u32[]{:S(2)}) copy-start(bf16[320,384]{1,0:T(8,128)(2,1)} %reshape.204) | copy-start | bytes 737284
  294.2 10.9 %copy-start.24 = (bf16[320,384]{1,0:T(8,128)(2,1)S(1)}, bf16[320,384]{1,0:T(8,128)(2,1)}, u32[]{:S(2)}) copy-start(bf16[320,384]{1,0:T(8,128)(2,1)} %reshape.203) | copy-start | bytes 737284
  294.2 14.3 %copy-start.12 = (bf16[320,384]{1,0:T(8,128)(2,1)S(1)}, bf16[320,384]{1,0:T(8,128)(2,1)}, u32[]{:S(2)}) copy-start(bf16[320,384]{1,0:T(8,128)(2,1)} %reshape.207) | copy-start | bytes 737284
  295.8 13.0 %copy-start.20 = (bf16[320,384]{1,0:T(8,128)(2,1)S(1)}, bf16[320,384]{1,0:T(8,128)(2,1)}, u32[]{:S(2)}) copy-start(bf16[320,384]{1,0:T(8,128)(2,1)} %reshape.208) | copy-start | bytes 737284
  314.7 7.8 %collective-permute-start.20 = (bf16[2,8,10,384]{3,2,1,0:T(8,128)(2,1)S(1)}, bf16[2,8,10,384]{3,2,1,0:T(8,128)(2,1)S(1)}, u32[]{:S(2)}, u32[]{:S(2)}) collective-permute-start(bf16[2,8,10,384]{3,2,1,0:T(8,128)(2,1)S(1)} %slice.566), channel_id=1, source_target_pairs={{0,64},{64,128},{128,192},{1,65},{65,129},{129,193},{2,66},{66,130... | collective-permute-start | bytes 368648 | tf_op jit(solution)/shard_map/ppermute | solution.py:25
  322.6 6.3 %collective-permute-start.21 = (bf16[6,1,10,384]{3,2,1,0:T(8,128)(2,1)S(1)}, bf16[6,1,10,384]{3,2,1,0:T(8,128)(2,1)S(1)}, u32[]{:S(2)}, u32[]{:S(2)}) collective-permute-start(bf16[6,1,10,384]{3,2,1,0:T(8,128)(2,1)S(1)} %get-tuple-element.66), channel_id=1, source_target_pairs={{0,16},{16,32},{32,48},{1,17},{17,33},{33,49},{2,18},{18,34},{34,5... | collective-permute-start | bytes 138248 | tf_op jit(solution)/shard_map/ppermute | solution.py:35
  325.7 5.1 %collective-permute-start.22 = (bf16[6,1,10,384]{3,2,1,0:T(8,128)(2,1)S(1)}, bf16[6,1,10,384]{3,2,1,0:T(8,128)(2,1)S(1)}, u32[]{:S(2)}, u32[]{:S(2)}) collective-permute-start(bf16[6,1,10,384]{3,2,1,0:T(8,128)(2,1)S(1)} %get-tuple-element.67), channel_id=1, source_target_pairs={{16,0},{32,16},{48,32},{17,1},{33,17},{49,33},{18,2},{34,18},{50,3... | collective-permute-start | bytes 138248 | tf_op jit(solution)/shard_map/ppermute | solution.py:36
  328.9 12.0 %copy-start.27 = (bf16[6,1,10,384]{3,2,1,0:T(8,128)(2,1)}, bf16[6,1,10,384]{3,2,1,0:T(8,128)(2,1)S(1)}, u32[]{:S(2)}) copy-start(bf16[6,1,10,384]{3,2,1,0:T(8,128)(2,1)S(1)} %collective-permute-done.21) | copy-start | bytes 138244
  333.2 15.9 %collective-permute-start.23 = (bf16[6,10,1,384]{3,2,1,0:T(2,128)(2,1)}, bf16[6,10,1,384]{3,2,1,0:T(2,128)(2,1)}, u32[]{:S(2)}, u32[]{:S(2)}) collective-permute-start(bf16[6,10,1,384]{3,2,1,0:T(2,128)(2,1)} %get-tuple-element.26), channel_id=1, source_target_pairs={{0,1},{1,2},{2,3},{3,4},{4,5},{5,6},{6,7},{7,8},{8,9},{9,10},{10,1... | collective-permute-start | bytes 138248 | tf_op jit(solution)/shard_map/ppermute | solution.py:35
  335.2 14.0 %collective-permute-start.39 = (bf16[6,10,1,384]{3,2,1,0:T(2,128)(2,1)}, bf16[6,10,1,384]{3,2,1,0:T(2,128)(2,1)}, u32[]{:S(2)}, u32[]{:S(2)}) collective-permute-start(bf16[6,10,1,384]{3,2,1,0:T(2,128)(2,1)} %get-tuple-element.27), channel_id=1, source_target_pairs={{1,0},{2,1},{3,2},{4,3},{5,4},{6,5},{7,6},{8,7},{9,8},{10,9},{11,1... | collective-permute-start | bytes 138248 | tf_op jit(solution)/shard_map/ppermute | solution.py:36
  356.3 21.7 %copy-start.3 = (bf16[4,8,10,384]{3,2,1,0:T(8,128)(2,1)S(1)}, bf16[4,8,10,384]{3,2,1,0:T(8,128)(2,1)}, u32[]{:S(2)}) copy-start(bf16[4,8,10,384]{3,2,1,0:T(8,128)(2,1)} %get-tuple-element.7) | copy-start | bytes 737284
  356.3 21.9 %copy-start.2 = (bf16[4,8,10,384]{3,2,1,0:T(8,128)(2,1)S(1)}, bf16[4,8,10,384]{3,2,1,0:T(8,128)(2,1)}, u32[]{:S(2)}) copy-start(bf16[4,8,10,384]{3,2,1,0:T(8,128)(2,1)} %get-tuple-element.6) | copy-start | bytes 737284
  378.0 15.1 %copy-start.13 = (bf16[320,384]{1,0:T(8,128)(2,1)S(1)}, bf16[320,384]{1,0:T(8,128)(2,1)}, u32[]{:S(2)}) copy-start(bf16[320,384]{1,0:T(8,128)(2,1)} %reshape.235) | copy-start | bytes 737284
  378.2 16.1 %slice-start = ((s8[7962624]{0:T(1024)(128)(4,1)}), s8[4194304]{0:T(1024)(128)(4,1)S(1)}, s32[]{:S(2)}) async-start(s8[7962624]{0:T(1024)(128)(4,1)} %bitcast.217), calls=%async_computation.2 | async-start | bytes 8388608
  378.3 16.1 %copy-start.23 = (bf16[320,384]{1,0:T(8,128)(2,1)S(1)}, bf16[320,384]{1,0:T(8,128)(2,1)}, u32[]{:S(2)}) copy-start(bf16[320,384]{1,0:T(8,128)(2,1)} %reshape.236) | copy-start | bytes 737284
  381.3 13.5 %copy-start.22 = (bf16[320,384]{1,0:T(8,128)(2,1)S(1)}, bf16[320,384]{1,0:T(8,128)(2,1)}, u32[]{:S(2)}) copy-start(bf16[320,384]{1,0:T(8,128)(2,1)} %reshape.237) | copy-start | bytes 737284
  382.7 12.4 %copy-start.25 = (bf16[320,384]{1,0:T(8,128)(2,1)S(1)}, bf16[320,384]{1,0:T(8,128)(2,1)}, u32[]{:S(2)}) copy-start(bf16[320,384]{1,0:T(8,128)(2,1)} %reshape.238) | copy-start | bytes 737284
  384.2 11.3 %copy-start.21 = (bf16[320,384]{1,0:T(8,128)(2,1)S(1)}, bf16[320,384]{1,0:T(8,128)(2,1)}, u32[]{:S(2)}) copy-start(bf16[320,384]{1,0:T(8,128)(2,1)} %reshape.240) | copy-start | bytes 737284
  385.7 10.2 %copy-start.11 = (bf16[320,384]{1,0:T(8,128)(2,1)S(1)}, bf16[320,384]{1,0:T(8,128)(2,1)}, u32[]{:S(2)}) copy-start(bf16[320,384]{1,0:T(8,128)(2,1)} %reshape.241) | copy-start | bytes 737284
  (28 other events, 127.5 us)
Sparse Core Ops, SparseCore 0:
  123.9 87.0 all-gather.2
  239.2 87.0 all-gather.4
